TPU v7x, 32 devices: a whole 2x2x4 slice. The times are simulated.
32 devices in a mesh: row: 8 (over z, y), col: 4 (over x, core).
Axes of the slice: x: 2, y: 2, z: 4, core: 2. Of those that a mesh axis runs over, the one named last changes fastest.
Arguments:
- trailing_matrix: float32 [2048, 2048], P('row', 'col'), may hold values from -24 to 1024, as said below
- rhs_block: float32 [2048, 128], P('row'), may hold values from -144 to 144
Outputs:
- factored: float32 [2048, 2048], P('row', 'col')
- solved_rhs: float32 [2048, 128], P('row')
Inputs may be any that keep to these rules, and one draw needn't show every extreme that they name: `trailing_matrix`: symmetric in logical order; its leading 2 * 256 by 512 logical block is positive definite.
All inputs are finite; a program needn't handle non-finite values.
Results may differ from a plain program's by a relative error of at most 0.00011.
Values sent between devices are 32-bit elements; how exact they have to be, the bound alone decides.
A program may use at most 64 MiB of HBM per device.

v0:
```python
import jax
import jax.numpy as jnp
from jax import lax
from jax.sharding import PartitionSpec as P

NB = 256


highest = lax.Precision.HIGHEST


def from_root(block, axis, source):
    block = jnp.where(lax.axis_index(axis) == source, block, jnp.zeros_like(block))
    return lax.psum(block, axis)


def lower_solve(factor, block_vals):
    return jax.scipy.linalg.solve_triangular(factor, block_vals, lower=True)


def per_device(trailing_matrix, rhs_block):
    rows_count = lax.axis_size("row")
    cols_count = lax.axis_size("col")
    row_index = lax.axis_index("row")
    col_index = lax.axis_index("col")
    tile_rows = trailing_matrix.shape[0] // NB
    tile_cols = trailing_matrix.shape[1] // NB
    tile_grid = trailing_matrix.reshape(tile_rows, NB, tile_cols, NB)
    rhs_tiles = rhs_block.reshape(tile_rows, NB, rhs_block.shape[1])
    row_ids = row_index + rows_count * jnp.arange(tile_rows, dtype=jnp.int32)
    col_ids = col_index + cols_count * jnp.arange(tile_cols, dtype=jnp.int32)

    def factor_panel(section, column, rhs_now):
        slot_idx = section // rows_count
        root_row = section % rows_count
        root_col = section % cols_count
        pivot_tile, pivot_rhs = (
            from_root(column[slot_idx], ("row", "col"), root_row * cols_count + root_col),
            from_root(rhs_now[slot_idx], ("row", "col"), root_row * cols_count + root_col),
        )
        factor = jnp.linalg.cholesky(pivot_tile)
        solved = lower_solve(factor, pivot_rhs)
        stacked = column.transpose(2, 0, 1).reshape(NB, tile_rows * NB)
        below_rows = lower_solve(factor, stacked).reshape(NB, tile_rows, NB).transpose(1, 2, 0)
        local_panel = jnp.where(
            (row_ids > section)[:, None, None],
            below_rows,
            jnp.where((row_ids == section)[:, None, None], factor[None, :, :], 0.0),
        )
        panel_rows = from_root(local_panel, "col", root_col)

        def fetch_tile(col_slot, gathered):
            tile_col = col_index + cols_count * col_slot
            piece = lax.dynamic_index_in_dim(panel_rows, tile_col // rows_count, 0, keepdims=False)
            received = from_root(piece, "row", tile_col % rows_count)
            return lax.dynamic_update_index_in_dim(gathered, received, col_slot, 0)

        column_tiles = lax.fori_loop(
            0, tile_cols, fetch_tile, jnp.zeros((tile_cols, NB, NB), jnp.float32)
        )
        update_rhs = jnp.einsum(
            "sab,sbn->san",
            panel_rows,
            jnp.broadcast_to(solved, (tile_rows,) + solved.shape),
            precision=highest,
        )
        rhs_now = jnp.where((row_ids > section)[:, None, None], rhs_now - update_rhs, rhs_now)
        rhs_now = jnp.where((row_ids == section)[:, None, None], solved[None, :, :], rhs_now)
        return (panel_rows, column_tiles, rhs_now)

    def trailing(section, part_grid, panel_rows, column_tiles, part_ids):
        product = jnp.einsum("sab,tcb->satc", panel_rows, column_tiles, precision=highest)
        inner_mask = (row_ids > section)[:, None, None, None] & (part_ids > section)[
            None, None, :, None
        ]
        part_grid = jnp.where(inner_mask, part_grid - product, part_grid)
        part_grid = jnp.where(
            (part_ids == section)[None, None, :, None], panel_rows[:, :, None, :], part_grid
        )
        zero_mask = (row_ids == section)[:, None, None, None] & (part_ids > section)[
            None, None, :, None
        ]
        return jnp.where(zero_mask, 0.0, part_grid)

    rows_first, cols_first, rhs_tiles = factor_panel(0, tile_grid[:, :, 0, :], rhs_tiles)
    tile_grid = trailing(0, tile_grid, rows_first, cols_first, col_ids)
    rows_second, cols_second, rhs_tiles = factor_panel(1, tile_grid[:, :, 0, :], rhs_tiles)
    tile_grid = trailing(1, tile_grid, rows_second, cols_second, col_ids)
    return (tile_grid.reshape(trailing_matrix.shape), rhs_tiles.reshape(rhs_block.shape))


def solution(mesh):
    placed = (P("row", "col"), P("row", None))
    return jax.shard_map(
        per_device,
        mesh=mesh,
        in_specs=placed,
        out_specs=(P("row", "col"), P("row", None)),
        check_vma=False,
    )
```

profile of v0, /device:TPU:30, one launch (start us, length us, event | category | flops | bytes accessed | tf_op | source)
XLA Modules:
  0.0 783.6 jit_solution(5220408088477425120)
XLA Ops:
  7.2 1.2 copy.4
  8.5 0.7 select_bitcast_fusion.1
  10.2 130.6 %all-reduce.16.cloned.1.call-done = (f32[256,256]{0,1:T(8,128)}, f32[256,128]{1,0:T(8,128)}) async-done(((f32[256,256]{0,1:T(8,128)}, f32[256,128]{1,0:T(8,128)}), (f32[256,256]{0,1:T(8,128)}, f32[256,128]{1,0:T(8,128)})) %all-reduce.16.cloned.1.call-update) | async-done | bytes 393232 | tf_op jit(solution)/shard_map/psum | solution.py:14
  140.8 1.1 copy.5
  142.0 11.7 %cholesky.130 = f32[128,128]{1,0:T(8,128)S(1)} custom-call(f32[128,128]{1,0:T(8,128)S(1)} %cholesky.194), custom_call_target="Cholesky" | custom-call | tf_op jit(solution)/shard_map/jit(cholesky)/cholesky | solution.py:41
  153.8 9.8 %custom-call.17 = f32[1,128,128]{1,2,0:T(8,128)S(1)} custom-call(f32[1,128,128]{2,1,0:T(8,128)S(1)} %get-tuple-element.314), custom_call_target="InvertDiagBlocksLowerTriangular" | custom-call | tf_op jit(solution)/shard_map/jit(cholesky)/cholesky | solution.py:41
  164.1 11.7 %cholesky.147 = f32[128,128]{1,0:T(8,128)S(1)} custom-call(f32[128,128]{1,0:T(8,128)S(1)} %convolution_subtract_fusion.9), custom_call_target="Cholesky" | custom-call | tf_op jit(solution)/shard_map/jit(cholesky)/cholesky | solution.py:41
  177.9 4.2 while.40
  178.7 1.4 bitcast_dynamic-update-slice_fusion.4
  180.7 1.4 bitcast_dynamic-update-slice_fusion.4
  182.1 19.7 %custom-call.18 = f32[2,128,128]{1,2,0:T(8,128)S(1)} custom-call(f32[2,128,128]{2,1,0:T(8,128)S(1)} %get-tuple-element.257), custom_call_target="InvertDiagBlocksLowerTriangular" | custom-call | tf_op jit(solution)/shard_map/jit(_solve_triangular)/triangular_solve | solution.py:18
  202.5 0.8 copy-done.5
  204.2 0.8 fusion.11
  205.2 31.7 %all-reduce.10.cloned.1.call-done = f32[1,256,256]{2,1,0:T(8,128)} async-done(((f32[1,256,256]{2,1,0:T(8,128)}), f32[1,256,256]{2,1,0:T(8,128)}) %all-reduce.10.cloned.1.call-update) | async-done | bytes 262160 | tf_op jit(solution)/shard_map/psum | solution.py:14
  236.9 1.1 copy.8
  238.0 0.9 copy-done.1
  238.9 151.0 %while.38 = (s32[]{:T(128)}, f32[2,256,256]{2,1,0:T(8,128)S(1)}, s32[]{:T(128)}, f32[1,256,256]{2,1,0:T(8,128)S(1)}, s32[]{:T(128)}, /*index=5*/u32[]{:T(128)}, ...) while((s32[]{:T(128)}, f32[2,256,256]{2,1,0:T(8,128)S(1)}, s32[]{:T(128)}, ...), condition=%wide.region_8.11_spmd, body=%wide.region_6.10_spmd.sunk | while | flops 131091 | bytes 2621776 | solution.py:58
  238.9 0.7 broadcast_select_fusion.6
  239.7 73.9 %all-reduce.18.cloned.1.call-done = f32[1,256,256]{2,1,0:T(8,128)} async-done(((f32[1,256,256]{2,1,0:T(8,128)}), f32[1,256,256]{2,1,0:T(8,128)}) %all-reduce.18.cloned.1.call-update) | async-done | bytes 262160 | tf_op jit(solution)/shard_map/while/body/eval_jaxpr/psum | solution.py:14
  313.6 1.0 constant_dynamic-update-slice_fusion.8
  314.7 0.7 broadcast_select_fusion.6
  315.4 73.5 %all-reduce.18.cloned.1.call-done = f32[1,256,256]{2,1,0:T(8,128)} async-done(((f32[1,256,256]{2,1,0:T(8,128)}), f32[1,256,256]{2,1,0:T(8,128)}) %all-reduce.18.cloned.1.call-update) | async-done | bytes 262160 | tf_op jit(solution)/shard_map/while/body/eval_jaxpr/psum | solution.py:14
  388.9 1.0 constant_dynamic-update-slice_fusion.8
  390.6 0.7 select_bitcast_fusion
  391.3 1.0 broadcast_select_fusion.2
  392.5 130.8 %all-reduce.14.cloned.1.call-done = (f32[256,256]{0,1:T(8,128)}, f32[256,128]{1,0:T(8,128)}) async-done(((f32[256,256]{0,1:T(8,128)}, f32[256,128]{1,0:T(8,128)}), (f32[256,256]{0,1:T(8,128)}, f32[256,128]{1,0:T(8,128)})) %all-reduce.14.cloned.1.call-update) | async-done | bytes 393232 | tf_op jit(solution)/shard_map/psum | solution.py:14
  523.3 1.1 copy.10
  524.5 11.7 %cholesky.164 = f32[128,128]{1,0:T(8,128)S(1)} custom-call(f32[128,128]{1,0:T(8,128)S(1)} %cholesky.197), custom_call_target="Cholesky" | custom-call | tf_op jit(solution)/shard_map/jit(cholesky)/cholesky | solution.py:41
  536.3 9.8 %custom-call.19 = f32[1,128,128]{1,2,0:T(8,128)S(1)} custom-call(f32[1,128,128]{2,1,0:T(8,128)S(1)} %get-tuple-element.310), custom_call_target="InvertDiagBlocksLowerTriangular" | custom-call | tf_op jit(solution)/shard_map/jit(cholesky)/cholesky | solution.py:41
  546.6 11.7 %cholesky.181 = f32[128,128]{1,0:T(8,128)S(1)} custom-call(f32[128,128]{1,0:T(8,128)S(1)} %convolution_subtract_fusion.8), custom_call_target="Cholesky" | custom-call | tf_op jit(solution)/shard_map/jit(cholesky)/cholesky | solution.py:41
  561.0 4.2 while.41
  561.8 1.4 bitcast_dynamic-update-slice_fusion.5
  563.8 1.4 bitcast_dynamic-update-slice_fusion.5
  565.2 19.7 %custom-call.20 = f32[2,128,128]{1,2,0:T(8,128)S(1)} custom-call(f32[2,128,128]{2,1,0:T(8,128)S(1)} %get-tuple-element.258), custom_call_target="InvertDiagBlocksLowerTriangular" | custom-call | tf_op jit(solution)/shard_map/jit(_solve_triangular)/triangular_solve | solution.py:18
  585.6 0.8 copy-done.6
  587.3 0.8 fusion.13
  588.4 31.7 %all-reduce.12.cloned.1.call-done = f32[1,256,256]{2,1,0:T(8,128)} async-done(((f32[1,256,256]{2,1,0:T(8,128)}), f32[1,256,256]{2,1,0:T(8,128)}) %all-reduce.12.cloned.1.call-update) | async-done | bytes 262160 | tf_op jit(solution)/shard_map/psum | solution.py:14
  620.0 1.1 copy.13
  621.2 0.9 copy-done
  622.1 152.0 %while.39 = (s32[]{:T(128)}, f32[2,256,256]{2,1,0:T(8,128)S(1)}, s32[]{:T(128)}, f32[1,256,256]{2,1,0:T(8,128)S(1)}, s32[]{:T(128)}, /*index=5*/u32[]{:T(128)}, ...) while((s32[]{:T(128)}, f32[2,256,256]{2,1,0:T(8,128)S(1)}, s32[]{:T(128)}, ...), condition=%wide.region_13.16_spmd, body=%wide.region_11.15_spmd.sunk | while | flops 131091 | bytes 2621776 | solution.py:58
  622.1 0.7 broadcast_select_fusion.7
  622.8 74.3 %all-reduce.20.cloned.1.call-done = f32[1,256,256]{2,1,0:T(8,128)} async-done(((f32[1,256,256]{2,1,0:T(8,128)}), f32[1,256,256]{2,1,0:T(8,128)}) %all-reduce.20.cloned.1.call-update) | async-done | bytes 262160 | tf_op jit(solution)/shard_map/while/body/eval_jaxpr/psum | solution.py:14
  697.2 1.0 constant_dynamic-update-slice_fusion.9
  698.2 0.7 broadcast_select_fusion.7
  699.0 74.2 %all-reduce.20.cloned.1.call-done = f32[1,256,256]{2,1,0:T(8,128)} async-done(((f32[1,256,256]{2,1,0:T(8,128)}), f32[1,256,256]{2,1,0:T(8,128)}) %all-reduce.20.cloned.1.call-update) | async-done | bytes 262160 | tf_op jit(solution)/shard_map/while/body/eval_jaxpr/psum | solution.py:14
  773.1 1.0 constant_dynamic-update-slice_fusion.9
  774.7 1.0 copy.14
  775.7 1.0 fusion.7
  (80 shorter events, 11.9 us)
Async XLA Ops:
  7.2 133.6 %all-reduce.16.cloned.1.call-start = ((), (), s32[]{:S(2)}) async-start(), calls=%async_computation.3 | async-start | bytes 786432 | tf_op jit(solution)/shard_map/psum | solution.py:14
  8.5 0.9 copy-start.4
  10.1 226.8 %all-reduce.10.cloned.1.call-start = ((), (), s32[]{:S(2)}) async-start(), calls=%async_computation | async-start | bytes 524288 | tf_op jit(solution)/shard_map/psum | solution.py:14
  140.8 1.2 copy-start.2
  202.4 0.9 copy-start.5
  238.0 1.0 copy-start.1
  238.9 74.7 %all-reduce.18.cloned.1.call-start = ((), (), s32[]{:S(2)}) async-start(), calls=%async_computation.4 | async-start | bytes 524288 | tf_op jit(solution)/shard_map/while/body/eval_jaxpr/psum | solution.py:14
  314.6 74.3 %all-reduce.18.cloned.1.call-start = ((), (), s32[]{:S(2)}) async-start(), calls=%async_computation.4 | async-start | bytes 524288 | tf_op jit(solution)/shard_map/while/body/eval_jaxpr/psum | solution.py:14
  389.9 133.4 %all-reduce.14.cloned.1.call-start = ((), (), s32[]{:S(2)}) async-start(), calls=%async_computation.2 | async-start | bytes 786432 | tf_op jit(solution)/shard_map/psum | solution.py:14
  392.4 227.7 %all-reduce.12.cloned.1.call-start = ((), (), s32[]{:S(2)}) async-start(), calls=%async_computation.1 | async-start | bytes 524288 | tf_op jit(solution)/shard_map/psum | solution.py:14
  523.3 1.2 copy-start.3
  585.5 0.9 copy-start.6
  621.1 1.0 copy-start
  622.1 75.1 %all-reduce.20.cloned.1.call-start = ((), (), s32[]{:S(2)}) async-start(), calls=%async_computation.5 | async-start | bytes 524288 | tf_op jit(solution)/shard_map/while/body/eval_jaxpr/psum | solution.py:14
  698.1 75.0 %all-reduce.20.cloned.1.call-start = ((), (), s32[]{:S(2)}) async-start(), calls=%async_computation.5 | async-start | bytes 524288 | tf_op jit(solution)/shard_map/while/body/eval_jaxpr/psum | solution.py:14
Sparse Core Ops, SparseCore 0:
  13.9 126.7 all-reduce.15
  205.1 31.8 all-reduce.9
  243.7 69.9 all-reduce.17
  319.1 69.8 all-reduce.17
  396.4 126.8 all-reduce.13
  588.2 31.8 all-reduce.11
  627.2 69.9 all-reduce.19
  703.3 69.8 all-reduce.19
where the time goes:
time: 788 us; the launch traced here: 784 us
  waiting for transfers between devices  621 us (79%)
  other arithmetic  115 us (15%)
  local copies, waits for them, and re-layouts  22.4 us (3%)
  between operations  17.1 us (2%)
    psum x8, waiting for transfers between devices, from_root(): return lax.psum(block, axis)  621 us
    another operation x13, other arithmetic, factor_panel(): factor = jnp.linalg.cholesky(pivot_tile)  68.5 us
    another operation x5, other arithmetic, lower_solve(): return jax.scipy.linalg.solve_triangular(factor, block_vals, lower=True)  39.4 us
  transfers between devices with their start and end apart: 8, of which 8 were waited for; matrix products, arithmetic and copies ran while one was open for 0% of the time, Pallas kernels for 0%

commit v1 on v0

v1 whole, which is shorter than its diff:
```python
import functools

import jax
import jax.numpy as jnp
from jax import lax
from jax.experimental import pallas as pl
from jax.experimental.pallas import tpu as pltpu
from jax.sharding import PartitionSpec as P

NB = 256
HB = 128
LEAD = 2 * NB
MESH = pl.DeviceIdType.MESH
highest = lax.Precision.HIGHEST


def dot(a, b):
    return jnp.dot(a, b, precision=highest, preferred_element_type=jnp.float32)


def dot_nt(a, b):
    return lax.dot_general(
        a, b, (((1,), (1,)), ((), ())), precision=highest, preferred_element_type=jnp.float32
    )


def exchange_kernel(
    n_row, n_col, a_ref, b_ref, rows_ref, lead_ref, cols_ref, rhs_ref, send_sem, recv_sem
):
    r = lax.axis_index("row")
    c = lax.axis_index("col")

    def at(axis, index):
        return (index, c) if axis == "row" else (r, index)

    axes = (("row", r, n_row), ("col", c, n_col))
    barrier = pltpu.get_barrier_semaphore()
    for axis, me, size in axes:
        pl.semaphore_signal(barrier, inc=1, device_id=at(axis, me + 1 - 2 * (me % 2)), device_id_type=MESH)

        @pl.when(me + 2 < size)
        def _():
            pl.semaphore_signal(barrier, inc=1, device_id=at(axis, me + 2), device_id_type=MESH)

        @pl.when(me >= 2)
        def _():
            pl.semaphore_signal(barrier, inc=1, device_id=at(axis, me - 2), device_id_type=MESH)

    peers = 2
    for axis, me, size in axes:
        peers += (me + 2 < size).astype(jnp.int32) + (me >= 2).astype(jnp.int32)
    pl.semaphore_wait(barrier, peers)

    def copy(ref, item, way, axis, target):
        return pltpu.make_async_remote_copy(
            src_ref=ref,
            dst_ref=ref,
            send_sem=send_sem.at[item, way],
            recv_sem=recv_sem.at[item],
            device_id=at(axis, target),
            device_id_type=MESH,
        )

    def forward(ref, item, axis, parity):
        _, me, size = axes[0] if axis == "row" else axes[1]

        @pl.when(jnp.logical_or(me % 2 != parity, me >= 2))
        def _():
            copy(ref, item, 0, axis, me).wait_recv()

        @pl.when(me % 2 == parity)
        def _():
            @pl.when(me + 2 < size)
            def _():
                copy(ref, item, 0, axis, me + 2).start()

            copy(ref, item, 1, axis, me + 1 - 2 * (me % 2)).start()

    def finish(ref, item, axis, parity):
        _, me, size = axes[0] if axis == "row" else axes[1]

        @pl.when(me % 2 == parity)
        def _():
            @pl.when(me + 2 < size)
            def _():
                copy(ref, item, 0, axis, me + 2).wait_send()

            copy(ref, item, 1, axis, me + 1 - 2 * (me % 2)).wait_send()

    for q in range(2):

        @pl.when(c == q)
        def _():
            rows_ref[q] = a_ref[:, :NB]

        @pl.when(r == q)
        def _():
            cols_ref[q] = a_ref[...]
            rhs_ref[q] = b_ref[...]

    halves = [pl.ds(0, HB), pl.ds(HB, HB)]
    across = [(rows_ref.at[q, half], "col", q) for half in halves for q in range(2)]
    down = [
        (lead_ref.at[0, halves[0]], "row", 0),
        (lead_ref.at[0, halves[1]], "row", 0),
        (lead_ref.at[1], "row", 0),
        (lead_ref.at[2], "row", 1),
    ]
    down += [(cols_ref.at[q, half], "row", q) for half in halves for q in range(2)]
    down += [(rhs_ref.at[q], "row", q) for q in range(2)]

    for item, (ref, axis, parity) in enumerate(across):
        forward(ref, item, axis, parity)

    @pl.when(r == 0)
    def _():
        lead_ref[0] = rows_ref[0]
        lead_ref[1] = rows_ref[1]

    @pl.when(r == 1)
    def _():
        lead_ref[2] = rows_ref[1]

    for item, (ref, axis, parity) in enumerate(down):
        forward(ref, item + len(across), axis, parity)
    for item, (ref, axis, parity) in enumerate(across + down):
        finish(ref, item, axis, parity)


EXCHANGE_ITEMS = 14


def exchange(n_row, n_col, a, b):
    vmem = pl.BlockSpec(memory_space=pltpu.VMEM)
    shapes = [(2, NB, NB), (3, NB, NB), (2,) + a.shape, (2,) + b.shape]
    return pl.pallas_call(
        functools.partial(exchange_kernel, n_row, n_col),
        out_shape=[jax.ShapeDtypeStruct(s, jnp.float32) for s in shapes],
        in_specs=[vmem] * 2,
        out_specs=[vmem] * 4,
        scratch_shapes=[
            pltpu.SemaphoreType.DMA((EXCHANGE_ITEMS, 2)),
            pltpu.SemaphoreType.DMA((EXCHANGE_ITEMS,)),
        ],
        compiler_params=pltpu.CompilerParams(
            collective_id=0, has_side_effects=True, vmem_limit_bytes=40 * 1024 * 1024
        ),
    )(a, b)


def rows_of(x, j):
    return jnp.broadcast_to(x[j : j + 1, :], x.shape)


def invert_factor(s):
    sub = lax.broadcasted_iota(jnp.int32, (8, HB), 0)
    lane = lax.broadcasted_iota(jnp.int32, (8, HB), 1)
    groups = len(s)
    t = [jnp.where(lane == sub + 8 * h, 1.0, 0.0).astype(jnp.float32) for h in range(groups)]
    done = []
    for g in range(groups):
        p, q, f = s[g], t[g], t[g]
        lanes = [jnp.broadcast_to(p[:, 8 * g + k : 8 * g + k + 1], (8, HB)) for k in range(8)]
        scale = jnp.ones((8, HB), jnp.float32)
        for j in range(8):
            here = sub == j
            pivot = rows_of(lanes[j], j)
            inv = 1.0 / pivot
            m = lanes[j] * inv
            for k in range(j + 1, 8):
                row = rows_of(lanes[k], j)
                lanes[k] = jnp.where(here, row * inv, lanes[k] - m * row)
            row = rows_of(p, j)
            p = jnp.where(here, row * inv, p - m * row)
            row = rows_of(q, j)
            q = jnp.where(here, row * inv, q - m * row)
            f = jnp.where(sub > j, f - m * rows_of(f, j), f)
            scale = jnp.where(here, pivot, scale)
        root = lax.rsqrt(scale)
        root = root * (1.5 - 0.5 * scale * root * root)
        done.append(f * root)
        if g + 1 < groups:
            prow = [rows_of(p, k) for k in range(8)]
            qrow = [rows_of(q, k) for k in range(8)]
        for h in range(g + 1, groups):
            lane_cols = [
                jnp.broadcast_to(s[h][:, 8 * g + k : 8 * g + k + 1], (8, HB)) for k in range(8)
            ]
            ps = [lane_cols[k] * prow[k] for k in range(8)]
            qs = [lane_cols[k] * qrow[k] for k in range(8)]
            s[h] = s[h] - (((ps[0] + ps[1]) + (ps[2] + ps[3])) + ((ps[4] + ps[5]) + (ps[6] + ps[7])))
            t[h] = t[h] - (((qs[0] + qs[1]) + (qs[2] + qs[3])) + ((qs[4] + qs[5]) + (qs[6] + qs[7])))
    return done


def factor_lead(s_ref, inv_ref):
    blocks = LEAD // HB

    def step(kb, carry):
        base = pl.multiple_of(kb * HB, HB)
        groups = [
            s_ref[pl.ds(pl.multiple_of(base + 8 * g, 8), 8), pl.ds(base, HB)] for g in range(HB // 8)
        ]
        li = jnp.concatenate(invert_factor(groups), axis=0)
        inv_ref[pl.ds(base, HB), pl.ds(base, HB)] = li
        for k in range(blocks):

            @pl.when(kb == k)
            def _():
                lo, hi = k * HB, (k + 1) * HB
                if k > 0:
                    inv_ref[lo:hi, :lo] = dot(li, inv_ref[lo:hi, :lo])
                if k + 1 < blocks:
                    u = dot(li, s_ref[lo:hi, hi:])
                    ut = u.T
                    s_ref[hi:, hi:] -= dot(ut, u)
                    inv_ref[hi:, :hi] -= dot(ut, inv_ref[lo:hi, :hi])

        return carry

    lax.fori_loop(0, blocks, step, 0)


def compute_kernel(
    n_col, a_ref, b_ref, rows_ref, lead_ref, cols_ref, rhs_ref, out_ref, y_ref, s_ref, inv_ref
):
    r = lax.axis_index("row")
    c = lax.axis_index("col")
    s_ref[:NB, :NB] = lead_ref[0]
    s_ref[:NB, NB:] = lead_ref[1]
    s_ref[NB:, NB:] = lead_ref[2]
    inv_ref[...] = jnp.zeros_like(inv_ref)
    factor_lead(s_ref, inv_ref)

    panels = []
    for k in range(2):
        inv_rows = inv_ref[k * NB : (k + 1) * NB, : (k + 1) * NB]
        total = dot_nt(rows_ref[0], inv_rows[:, :NB])
        if k == 1:
            total += dot_nt(rows_ref[1], inv_rows[:, NB:])
        panels.append(total)
    tri = lax.broadcasted_iota(jnp.int32, (NB, NB), 0) >= lax.broadcasted_iota(jnp.int32, (NB, NB), 1)

    def solve(ref, cols):
        first = dot(inv_ref[:NB, :NB], ref[0, :, cols])
        second = dot(inv_ref[NB:, :NB], ref[0, :, cols]) + dot(inv_ref[NB:, NB:], ref[1, :, cols])
        return first, second

    y0, y1 = solve(rhs_ref, slice(None))
    updated = b_ref[...] - (dot(panels[0], y0) + dot(panels[1], y1))
    y_ref[...] = jnp.where(r == 0, y0, jnp.where(r == 1, y1, updated))
    for slot in range(a_ref.shape[1] // NB):
        cols = slice(slot * NB, (slot + 1) * NB)
        j = c + n_col * slot
        z0, z1 = solve(cols_ref, cols)
        inner = a_ref[:, cols] - (dot(panels[0], z0) + dot(panels[1], z1))
        inner = jnp.where(r >= 2, inner, 0.0)
        if slot == 0:
            panel = jnp.where(j == 0, panels[0], panels[1])
            keep = jnp.logical_or(r > j, jnp.logical_and(r == j, tri))
            inner = jnp.where(j >= 2, inner, jnp.where(keep, panel, 0.0))
        out_ref[:, cols] = inner


def compute(n_col, a, b, rows, lead, cols, rhs):
    vmem = pl.BlockSpec(memory_space=pltpu.VMEM)
    return pl.pallas_call(
        functools.partial(compute_kernel, n_col),
        out_shape=[jax.ShapeDtypeStruct(x.shape, jnp.float32) for x in (a, b)],
        in_specs=[vmem] * 6,
        out_specs=[vmem] * 2,
        scratch_shapes=[
            pltpu.VMEM((LEAD, LEAD), jnp.float32),
            pltpu.VMEM((LEAD, LEAD), jnp.float32),
        ],
        compiler_params=pltpu.CompilerParams(vmem_limit_bytes=40 * 1024 * 1024),
    )(a, b, rows, lead, cols, rhs)


def solution(mesh):
    n_row, n_col = mesh.shape["row"], mesh.shape["col"]

    def per_device(a, b):
        return tuple(compute(n_col, a, b, *exchange(n_row, n_col, a, b)))

    placed = (P("row", "col"), P("row", None))
    return jax.shard_map(
        per_device, mesh=mesh, in_specs=placed, out_specs=placed, check_vma=False
    )
```

time: 788 us -> 107 us (0.14)
  waiting for transfers between devices: 621 us -> 0 us
  other arithmetic: 115 us -> 0 us
  Pallas kernels: 0 us -> 102 us
  local copies, waits for them, and re-layouts: 22.4 us -> 1.94 us
  between operations: 17.1 us -> 0.65 us
    psum x8 -> x0, waiting for transfers between devices: 621 us -> none  [from_root(): return lax.psum(block, axis)]
    another operation x18 -> x0, other arithmetic: 108 us -> none  [the longest x13 68.5 us: factor_panel(): factor = jnp.linalg.cholesky(pivot_tile)]
    pallas_call x0 -> x2, Pallas kernels: none -> 102 us  [the longest x1 73.7 us: exchange(): pl.pallas_call(functools.partial(exchange_kernel, n_row, n_col), out_shap...]
    another operation x23 -> x0, local copies, waits for them, and re-layouts: 8.29 us -> none  [the longest x17 8.17 us: lower_solve(): return jax.scipy.linalg.solve_triangular(factor, block_vals, lower=True)]
  transfers between devices with their start and end apart: 8 -> 0, of which waited for: 8 -> 0; matrix products, arithmetic and copies ran while one was open for 0% -> 0% of each run, Pallas kernels for 0% -> 0%
where the time goes in v1:
time: 107 us; the launch traced here: 105 us
  Pallas kernels  102 us (95%)
  local copies, waits for them, and re-layouts  1.94 us (2%)
    pallas_call x1, Pallas kernels, exchange(): pl.pallas_call(functools.partial(exchange_kernel, n_row, n_col), out_shap...  73.7 us
    pallas_call x1, Pallas kernels, compute(): pl.pallas_call(functools.partial(compute_kernel, n_col), out_shape=[jax.S...  28.4 us

profile of v1, /device:TPU:30, one launch (start us, length us, event | category | flops | bytes accessed | tf_op | source)
XLA Modules:
  0.0 104.7 jit_solution(16455743611084450982)
XLA Ops:
  0.6 0.0 copy-start
  0.6 1.0 copy-done
  1.7 0.0 copy-start.1
  1.7 0.9 copy-done.1
  2.6 73.7 %shard_map.41 = (f32[2,256,256]{2,1,0:T(8,128)S(1)}, f32[3,256,256]{2,1,0:T(8,128)S(1)}, f32[2,256,512]{2,1,0:T(8,128)S(1)}, f32[2,256,128]{2,1,0:T(8,128)S(1)}) custom-call(f32[256,512]{1,0:T(8,128)S(1)} %copy-done, f32[256,128]{1,0:T(8,128)S(1)} %copy-done.1), custom_call_target="tpu_custom_call" | custom-call | tf_op jit(solution)/shard_map/pallas_call | solution.py:136
  76.3 28.4 %shard_map.42 = (f32[256,512]{1,0:T(8,128)}, f32[256,128]{1,0:T(8,128)}) custom-call(f32[256,512]{1,0:T(8,128)S(1)} %copy-done, f32[256,128]{1,0:T(8,128)S(1)} %copy-done.1, f32[2,256,256]{2,1,0:T(8,128)S(1)} %get-tuple-element.6.rows_ref, f32[3,256,256]{2,1,0:T(8,128)S(1)} %get-tuple-element.7.lead_ref, f32[2,256,512]{2,1,0:T(8,128)S(1)} %get-tuple-element.8.cols_ref, ...), custom_call_target="tpu_custom_call" | custom-call | tf_op jit(solution)/shard_map/pallas_call | solution.py:267
Async XLA Ops:
  0.6 1.0 copy-start
  1.7 0.9 copy-start.1

commit v2 on v1

v2 whole, which is shorter than its diff:
```python
import functools

import jax
import jax.numpy as jnp
from jax import lax
from jax.experimental import pallas as pl
from jax.experimental.pallas import tpu as pltpu
from jax.sharding import PartitionSpec as P

NB = 256
HB = 128
LEAD = 2 * NB
MESH = pl.DeviceIdType.MESH
highest = lax.Precision.HIGHEST


def dot(a, b):
    return jnp.dot(a, b, precision=highest, preferred_element_type=jnp.float32)


def dot_nt(a, b):
    return lax.dot_general(
        a, b, (((1,), (1,)), ((), ())), precision=highest, preferred_element_type=jnp.float32
    )


class Exchange:
    def __init__(self, n_row, n_col, send_sem, recv_sem):
        self.r = lax.axis_index("row")
        self.c = lax.axis_index("col")
        self.axes = {"row": (self.r, n_row), "col": (self.c, n_col)}
        self.send_sem, self.recv_sem = send_sem, recv_sem
        self.started = []

    def at(self, axis, index):
        return (index, self.c) if axis == "row" else (self.r, index)

    def barrier(self):
        barrier = pltpu.get_barrier_semaphore()
        peers = 0
        for axis, (me, size) in self.axes.items():
            for there, target in (
                (None, me + 1 - 2 * (me % 2)),
                (me + 2 < size, me + 2),
                (me >= 2, me - 2),
            ):

                def signal():
                    pl.semaphore_signal(
                        barrier, inc=1, device_id=self.at(axis, target), device_id_type=MESH
                    )

                if there is None:
                    signal()
                    peers += 1
                else:
                    pl.when(there)(signal)
                    peers += there.astype(jnp.int32)
        pl.semaphore_wait(barrier, peers)

    def copy(self, ref, item, way, axis, target):
        return pltpu.make_async_remote_copy(
            src_ref=ref,
            dst_ref=ref,
            send_sem=self.send_sem.at[item, way],
            recv_sem=self.recv_sem.at[item],
            device_id=self.at(axis, target),
            device_id_type=MESH,
        )

    def forward(self, ref, axis, parity):
        me, size = self.axes[axis]
        item = len(self.started)
        self.started.append((ref, axis, parity))

        def run_send():
            @pl.when(me + 2 < size)
            def _():
                self.copy(ref, item, 0, axis, me + 2).start()

            self.copy(ref, item, 1, axis, me + 1 - 2 * (me % 2)).start()

        def from_source():
            @pl.when(me == parity)
            def _():
                run_send()

        def elsewhere():
            @pl.when(me != parity)
            def _():
                self.copy(ref, item, 0, axis, me).wait_recv()

                @pl.when(me % 2 == parity)
                def _():
                    run_send()

        return from_source, elsewhere

    def finish(self):
        for item, (ref, axis, parity) in enumerate(self.started):
            me, size = self.axes[axis]

            @pl.when(me % 2 == parity)
            def _():
                @pl.when(me + 2 < size)
                def _():
                    self.copy(ref, item, 0, axis, me + 2).wait_send()

                self.copy(ref, item, 1, axis, me + 1 - 2 * (me % 2)).wait_send()


LEAD_CHUNK = 64
ITEMS = 64
POINTS = 4


def plan_exchange(ex, a_ref, b_ref, rows_ref, lead_ref, cols_ref, rhs_ref):
    r, c = ex.r, ex.c
    width = a_ref.shape[1]
    rows_items = [ex.forward(rows_ref.at[q], "col", q) for q in range(2)]
    first = {}
    lead = {}
    chunks = NB // LEAD_CHUNK
    for k in range(chunks):
        part = pl.ds(k * LEAD_CHUNK, LEAD_CHUNK)
        for q in range(2):
            first[k, q] = ex.forward(cols_ref.at[q, part, pl.ds(0, NB)], "row", q)
        for n, owner in ((0, 0), (1, 1), (2, 1)):
            lead[k, n] = ex.forward(lead_ref.at[n, part], "col", owner)
    rest = [
        [
            ex.forward(cols_ref.at[q, pl.ds(h * HB, HB), pl.ds(NB, width - NB)], "row", q)
            for q in range(2)
        ]
        for h in range(2)
    ]
    rhs_items = [ex.forward(rhs_ref.at[q], "row", q) for q in range(2)]

    def start():
        for q in range(2):

            @pl.when(c == q)
            def _():
                rows_ref[q] = a_ref[:, :NB]

            @pl.when(r == q)
            def _():
                cols_ref[q] = a_ref[...]
                rhs_ref[q] = b_ref[...]

        for k in range(chunks):
            for q in range(2):
                first[k, q][0]()
        for item in rows_items:
            item[0]()
        for pair in rest:
            for item in pair:
                item[0]()
        for item in rhs_items:
            item[0]()

    def first_part(k):
        part = pl.ds(k * LEAD_CHUNK, LEAD_CHUNK)
        for q in range(2):
            first[k, q][1]()

            @pl.when(c == q)
            def _():
                lead_ref[q, part] = cols_ref[0, part, :NB]

            lead[k, q][0]()

        @pl.when(c == 1)
        def _():
            lead_ref[2, part] = cols_ref[1, part, :NB]

        lead[k, 2][0]()

    def lead_part(k):
        for n in range(3):
            lead[k, n][1]()

    def both(items):
        for item in items:
            item[1]()

    ahead = [start, lambda: first_part(0), lambda: first_part(1), lambda: lead_part(0), lambda: lead_part(1)]
    inside = {
        0: [lambda: first_part(2)],
        1: [lambda: first_part(3), lambda: lead_part(2)],
        2: [lambda: lead_part(3)],
        3: [lambda: both(rest[0])],
        4: [lambda: both(rows_items)],
        5: [lambda: both(rest[1])],
        7: [lambda: both(rhs_items)],
    }
    return ahead, inside


def rows_of(x, j):
    return jnp.broadcast_to(x[j : j + 1, :], x.shape)


def invert_factor(s, hook=lambda point: None):
    sub = lax.broadcasted_iota(jnp.int32, (8, HB), 0)
    lane = lax.broadcasted_iota(jnp.int32, (8, HB), 1)
    groups = len(s)
    t = [jnp.where(lane == sub + 8 * h, 1.0, 0.0).astype(jnp.float32) for h in range(groups)]
    done = []
    for g in range(groups):
        if g % (groups // POINTS) == 0:
            hook(g // (groups // POINTS))
        p, q, f = s[g], t[g], t[g]
        lanes = [jnp.broadcast_to(p[:, 8 * g + k : 8 * g + k + 1], (8, HB)) for k in range(8)]
        scale = jnp.ones((8, HB), jnp.float32)
        for j in range(8):
            here = sub == j
            pivot = rows_of(lanes[j], j)
            inv = 1.0 / pivot
            m = lanes[j] * inv
            for k in range(j + 1, 8):
                row = rows_of(lanes[k], j)
                lanes[k] = jnp.where(here, row * inv, lanes[k] - m * row)
            row = rows_of(p, j)
            p = jnp.where(here, row * inv, p - m * row)
            row = rows_of(q, j)
            q = jnp.where(here, row * inv, q - m * row)
            f = jnp.where(sub > j, f - m * rows_of(f, j), f)
            scale = jnp.where(here, pivot, scale)
        root = lax.rsqrt(scale)
        root = root * (1.5 - 0.5 * scale * root * root)
        done.append(f * root)
        if g + 1 < groups:
            prow = [rows_of(p, k) for k in range(8)]
            qrow = [rows_of(q, k) for k in range(8)]
        for h in range(g + 1, groups):
            lane_cols = [
                jnp.broadcast_to(s[h][:, 8 * g + k : 8 * g + k + 1], (8, HB)) for k in range(8)
            ]
            ps = [lane_cols[k] * prow[k] for k in range(8)]
            qs = [lane_cols[k] * qrow[k] for k in range(8)]
            s[h] = s[h] - (((ps[0] + ps[1]) + (ps[2] + ps[3])) + ((ps[4] + ps[5]) + (ps[6] + ps[7])))
            t[h] = t[h] - (((qs[0] + qs[1]) + (qs[2] + qs[3])) + ((qs[4] + qs[5]) + (qs[6] + qs[7])))
    return done


def factor_lead(lead_ref, s_ref, inv_ref, inside):
    blocks = LEAD // HB

    def step(kb, carry):
        def hook(point):
            for k in range(blocks):
                jobs = inside.get(k * POINTS + point)
                if jobs:

                    @pl.when(kb == k)
                    def _():
                        for job in jobs:
                            job()

        base = pl.multiple_of(kb * HB, HB)
        for k in range(blocks):

            @pl.when(kb == k)
            def _():
                rows = slice(k * HB, (k + 1) * HB)
                here = slice(k * HB % NB, k * HB % NB + HB)
                if k * HB < NB:
                    s_ref[rows, :NB] += lead_ref[0, here]
                    s_ref[rows, NB:] += lead_ref[1, here]
                else:
                    s_ref[rows, NB:] += lead_ref[2, here]

        groups = [
            s_ref[pl.ds(pl.multiple_of(base + 8 * g, 8), 8), pl.ds(base, HB)] for g in range(HB // 8)
        ]
        li = jnp.concatenate(invert_factor(groups, hook), axis=0)
        inv_ref[pl.ds(base, HB), pl.ds(base, HB)] = li
        for k in range(blocks):

            @pl.when(kb == k)
            def _():
                lo, hi = k * HB, (k + 1) * HB
                if k > 0:
                    inv_ref[lo:hi, :lo] = dot(li, inv_ref[lo:hi, :lo])
                if k + 1 < blocks:
                    u = dot(li, s_ref[lo:hi, hi:])
                    ut = u.T
                    s_ref[hi:, hi:] -= dot(ut, u)
                    inv_ref[hi:, :hi] -= dot(ut, inv_ref[lo:hi, :hi])

        return carry

    lax.fori_loop(0, blocks, step, 0)


def whole_kernel(
    n_row,
    n_col,
    a_ref,
    b_ref,
    out_ref,
    y_ref,
    rows_ref,
    lead_ref,
    cols_ref,
    rhs_ref,
    s_ref,
    inv_ref,
    send_sem,
    recv_sem,
):
    ex = Exchange(n_row, n_col, send_sem, recv_sem)
    r, c = ex.r, ex.c
    ex.barrier()
    ahead, inside = plan_exchange(ex, a_ref, b_ref, rows_ref, lead_ref, cols_ref, rhs_ref)
    ahead[0]()
    s_ref[...] = jnp.zeros_like(s_ref)
    inv_ref[...] = jnp.zeros_like(inv_ref)
    for job in ahead[1:]:
        job()
    factor_lead(lead_ref, s_ref, inv_ref, inside)

    panels = []
    for k in range(2):
        inv_rows = inv_ref[k * NB : (k + 1) * NB, : (k + 1) * NB]
        total = dot_nt(rows_ref[0], inv_rows[:, :NB])
        if k == 1:
            total += dot_nt(rows_ref[1], inv_rows[:, NB:])
        panels.append(total)
    tri = lax.broadcasted_iota(jnp.int32, (NB, NB), 0) >= lax.broadcasted_iota(jnp.int32, (NB, NB), 1)

    def solve(ref, cols):
        first = dot(inv_ref[:NB, :NB], ref[0, :, cols])
        second = dot(inv_ref[NB:, :NB], ref[0, :, cols]) + dot(inv_ref[NB:, NB:], ref[1, :, cols])
        return first, second

    y0, y1 = solve(rhs_ref, slice(None))
    updated = b_ref[...] - (dot(panels[0], y0) + dot(panels[1], y1))
    y_ref[...] = jnp.where(r == 0, y0, jnp.where(r == 1, y1, updated))
    for slot in range(a_ref.shape[1] // NB):
        cols = slice(slot * NB, (slot + 1) * NB)
        j = c + n_col * slot
        z0, z1 = solve(cols_ref, cols)
        inner = a_ref[:, cols] - (dot(panels[0], z0) + dot(panels[1], z1))
        inner = jnp.where(r >= 2, inner, 0.0)
        if slot == 0:
            panel = jnp.where(j == 0, panels[0], panels[1])
            keep = jnp.logical_or(r > j, jnp.logical_and(r == j, tri))
            inner = jnp.where(j >= 2, inner, jnp.where(keep, panel, 0.0))
        out_ref[:, cols] = inner
    ex.finish()


def whole(n_row, n_col, a, b):
    vmem = pl.BlockSpec(memory_space=pltpu.VMEM)
    shapes = [(2, NB, NB), (3, NB, NB), (2,) + a.shape, (2,) + b.shape, (LEAD, LEAD), (LEAD, LEAD)]
    return pl.pallas_call(
        functools.partial(whole_kernel, n_row, n_col),
        out_shape=[jax.ShapeDtypeStruct(x.shape, jnp.float32) for x in (a, b)],
        in_specs=[vmem] * 2,
        out_specs=[vmem] * 2,
        scratch_shapes=[pltpu.VMEM(s, jnp.float32) for s in shapes]
        + [pltpu.SemaphoreType.DMA((ITEMS, 2)), pltpu.SemaphoreType.DMA((ITEMS,))],
        compiler_params=pltpu.CompilerParams(
            collective_id=0, has_side_effects=True, vmem_limit_bytes=40 * 1024 * 1024
        ),
    )(a, b)


def solution(mesh):
    n_row, n_col = mesh.shape["row"], mesh.shape["col"]

    def per_device(a, b):
        return tuple(whole(n_row, n_col, a, b))

    placed = (P("row", "col"), P("row", None))
    return jax.shard_map(
        per_device, mesh=mesh, in_specs=placed, out_specs=placed, check_vma=False
    )
```

time: 107 us -> 104 us (0.972)
  the two profiles are of different devices: /device:TPU:30 before, /device:TPU:26 now
where the time goes in v2:
time: 104 us
  Pallas kernels  100 us (96%)
  local copies, waits for them, and re-layouts  3.39 us (3%)
    pallas_call x1, Pallas kernels, whole(): pl.pallas_call(functools.partial(whole_kernel, n_row, n_col), out_shape=[...  100 us
    unnamed x6, local copies, waits for them, and re-layouts  3.39 us

profile of v2, /device:TPU:26, one launch (start us, length us, event | category | flops | bytes accessed | tf_op | source)
XLA Modules:
  0.0 104.0 jit_solution(113433081025055479)
XLA Ops:
  0.6 0.0 copy-start
  0.6 1.0 copy-done
  1.7 0.0 copy-start.1
  1.7 0.9 copy-done.1
  2.6 100.0 %shard_map.41 = (f32[256,512]{1,0:T(8,128)S(1)}, f32[256,128]{1,0:T(8,128)S(1)}) custom-call(f32[256,512]{1,0:T(8,128)S(1)} %copy-done, f32[256,128]{1,0:T(8,128)S(1)} %copy-done.1), custom_call_target="tpu_custom_call" | custom-call | tf_op jit(solution)/shard_map/pallas_call | solution.py:358
  102.6 0.8 copy.6
  103.4 0.7 copy.7
Async XLA Ops:
  0.6 1.0 %copy-start = (f32[256,512]{1,0:T(8,128)S(1)}, f32[256,512]{1,0:T(8,128)}, u32[]{:S(2)}) copy-start(f32[256,512]{1,0:T(8,128)} %a_ref.1) | copy-start | bytes 1572868
  1.7 0.9 copy-start.1

commit v3 on v2

v3 whole, which is shorter than its diff:
```python
import functools

import jax
import jax.numpy as jnp
from jax import lax
from jax.experimental import pallas as pl
from jax.experimental.pallas import tpu as pltpu
from jax.sharding import PartitionSpec as P

NB = 256
HB = 128
LEAD = 2 * NB
MESH = pl.DeviceIdType.MESH
highest = lax.Precision.HIGHEST


def dot(a, b):
    return jnp.dot(a, b, precision=highest, preferred_element_type=jnp.float32)


def dot_nt(a, b):
    return lax.dot_general(
        a, b, (((1,), (1,)), ((), ())), precision=highest, preferred_element_type=jnp.float32
    )


class Exchange:
    def __init__(self, n_row, n_col, send_sem, recv_sem):
        self.r = lax.axis_index("row")
        self.c = lax.axis_index("col")
        self.axes = {"row": (self.r, n_row), "col": (self.c, n_col)}
        self.send_sem, self.recv_sem = send_sem, recv_sem
        self.items = 0
        self.sent = []

    def at(self, axis, index):
        return (index, self.c) if axis == "row" else (self.r, index)

    def barrier(self):
        barrier = pltpu.get_barrier_semaphore()
        peers = 0
        for axis, (me, size) in self.axes.items():
            for there, target in (
                (None, me + 1 - 2 * (me % 2)),
                (me + 2 < size, me + 2),
                (me >= 2, me - 2),
            ):

                def signal():
                    pl.semaphore_signal(
                        barrier, inc=1, device_id=self.at(axis, target), device_id_type=MESH
                    )

                if there is None:
                    signal()
                    peers += 1
                else:
                    pl.when(there)(signal)
                    peers += there.astype(jnp.int32)
        pl.semaphore_wait(barrier, peers)

    def copy(self, ref, item, way, axis, target):
        return pltpu.make_async_remote_copy(
            src_ref=ref,
            dst_ref=ref,
            send_sem=self.send_sem.at[item, way],
            recv_sem=self.recv_sem.at[item],
            device_id=self.at(axis, target),
            device_id_type=MESH,
        )

    def flow(self, ref, axis, source, low=0, active=True):
        me, size = self.axes[axis]
        item = self.items
        self.items += 1
        chain = jnp.logical_and(active, me % 2 == source % 2)
        sends = (
            (jnp.logical_and(chain, jnp.logical_and(me >= source, me + 2 < size)), me + 2),
            (jnp.logical_and(chain, jnp.logical_and(me <= source, me >= low + 2)), me - 2),
            (chain, me + 1 - 2 * (me % 2)),
        )

        def send():
            for way, (there, target) in enumerate(sends):

                @pl.when(there)
                def _():
                    self.copy(ref, item, way, axis, target).start()

        def wait_sent():
            for way, (there, target) in enumerate(sends):

                @pl.when(there)
                def _():
                    self.copy(ref, item, way, axis, target).wait_send()

        self.sent.append(wait_sent)

        def from_source():
            @pl.when(jnp.logical_and(active, me == source))
            def _():
                send()

        def elsewhere():
            @pl.when(jnp.logical_and(active, me != source))
            def _():
                self.copy(ref, item, 2, axis, me + 1 - 2 * (me % 2)).wait_recv()
                send()

        return from_source, elsewhere

    def finish(self):
        for wait_sent in self.sent:
            wait_sent()


ITEMS = 48
POINTS = 4
BLOCKS = LEAD // HB
UPPER = [(i, j) for i in range(BLOCKS) for j in range(i, BLOCKS)]
LEAD_ITEMS = [(0, 1, 0, 0), (1, 1, 0, 0), (2, 2, 0, 1), (4, 1, 0, 0), (5, 2, 0, 1), (7, 3, 1, 1)]


def plan_exchange(ex, n_col, slots, a_ref, b_ref, rows_ref, lead_ref, pan_ref, rhs_ref):
    r, c = ex.r, ex.c
    halves = [pl.ds(0, HB), pl.ds(HB, HB)]
    rows_items = [ex.flow(rows_ref.at[q], "col", q) for q in range(2)]
    lead = []
    for start, count, q, owner in LEAD_ITEMS:
        ref = lead_ref.at[pl.ds(start, count)]
        lead.append((ex.flow(ref, "row", q, active=c == owner), ex.flow(ref, "col", owner)))
    rhs = [
        (ex.flow(rhs_ref.at[q], "row", q, active=c == 2), ex.flow(rhs_ref.at[q], "col", 2))
        for q in range(2)
    ]
    pan = []
    for q in range(2):
        for half in halves:
            for t in range(slots):
                j = c + n_col * t
                active = jnp.logical_and(r >= 2, j >= 2)
                pan.append(ex.flow(pan_ref.at[t, q, half], "row", j, low=2, active=active))

    def start():
        for n, (i, j) in enumerate(UPPER):
            q, owner = i * HB // NB, j * HB // NB

            @pl.when(jnp.logical_and(r == q, c == owner))
            def _():
                lead_ref[n] = a_ref[i * HB % NB : i * HB % NB + HB, j * HB % NB : j * HB % NB + HB]

        for row_flow, _ in lead:
            row_flow[0]()
        for q in range(2):

            @pl.when(c == q)
            def _():
                rows_ref[q] = a_ref[:, :NB]

            rows_items[q][0]()

            @pl.when(jnp.logical_and(r == q, c == 2))
            def _():
                rhs_ref[q] = b_ref[...]

            rhs[q][0][0]()

    def pass_on(pair):
        pair[0][1]()
        pair[1][0]()

    def start_pan():
        for t in range(slots):

            @pl.when(jnp.logical_and(r >= 2, r == c + n_col * t))
            def _():
                pan_ref[t] = rows_ref[...]

        for item in pan:
            item[0]()

    inside = {}

    def put(point, *jobs):
        inside.setdefault(point, []).extend(jobs)

    def along_row(n):
        return lambda: pass_on(lead[n])

    def along_col(n):
        return lead[n][1][1]

    ahead = [start, along_row(0), along_col(0)]
    put(0, along_row(1), along_row(2))
    put(1, along_col(1), along_col(2), rows_items[0][1], rows_items[1][1], start_pan)
    put(2, along_row(3), along_row(4))
    put(3, along_col(3), along_col(4))
    put(4, along_row(5))
    put(5, along_col(5))
    put(6, lambda: pass_on(rhs[0]), lambda: pass_on(rhs[1]))
    put(8, rhs[0][1][1], rhs[1][1][1])
    for n, item in enumerate(pan):
        put(5 + n * 8 // len(pan), item[1])
    return ahead, inside


def rows_of(x, j):
    return jnp.broadcast_to(x[j : j + 1, :], x.shape)


def invert_factor(s, hook=lambda point: None):
    sub = lax.broadcasted_iota(jnp.int32, (8, HB), 0)
    lane = lax.broadcasted_iota(jnp.int32, (8, HB), 1)
    groups = len(s)
    t = [jnp.where(lane == sub + 8 * h, 1.0, 0.0).astype(jnp.float32) for h in range(groups)]
    done = []
    for g in range(groups):
        if g % (groups // POINTS) == 0:
            hook(g // (groups // POINTS))
        p, q, f = s[g], t[g], t[g]
        lanes = [jnp.broadcast_to(p[:, 8 * g + k : 8 * g + k + 1], (8, HB)) for k in range(8)]
        scale = jnp.ones((8, HB), jnp.float32)
        for j in range(8):
            here = sub == j
            pivot = rows_of(lanes[j], j)
            inv = 1.0 / pivot
            m = lanes[j] * inv
            for k in range(j + 1, 8):
                row = rows_of(lanes[k], j)
                lanes[k] = jnp.where(here, row * inv, lanes[k] - m * row)
            row = rows_of(p, j)
            p = jnp.where(here, row * inv, p - m * row)
            row = rows_of(q, j)
            q = jnp.where(here, row * inv, q - m * row)
            f = jnp.where(sub > j, f - m * rows_of(f, j), f)
            scale = jnp.where(here, pivot, scale)
        root = lax.rsqrt(scale)
        root = root * (1.5 - 0.5 * scale * root * root)
        done.append(f * root)
        if g + 1 < groups:
            prow = [rows_of(p, k) for k in range(8)]
            qrow = [rows_of(q, k) for k in range(8)]
        for h in range(g + 1, groups):
            lane_cols = [
                jnp.broadcast_to(s[h][:, 8 * g + k : 8 * g + k + 1], (8, HB)) for k in range(8)
            ]
            ps = [lane_cols[k] * prow[k] for k in range(8)]
            qs = [lane_cols[k] * qrow[k] for k in range(8)]
            s[h] = s[h] - (((ps[0] + ps[1]) + (ps[2] + ps[3])) + ((ps[4] + ps[5]) + (ps[6] + ps[7])))
            t[h] = t[h] - (((qs[0] + qs[1]) + (qs[2] + qs[3])) + ((qs[4] + qs[5]) + (qs[6] + qs[7])))
    return done


def factor_lead(lead_ref, s_ref, inv_ref, inside):
    blocks = BLOCKS

    def step(kb, carry):
        def hook(point):
            for k in range(blocks):
                jobs = inside.get(k * POINTS + point)
                if jobs:

                    @pl.when(kb == k)
                    def _():
                        for job in jobs:
                            job()

        base = pl.multiple_of(kb * HB, HB)
        for k in range(blocks):

            @pl.when(kb == k)
            def _():
                rows = slice(k * HB, (k + 1) * HB)
                s_ref[rows, rows] += lead_ref[UPPER.index((k, k))]

        groups = [
            s_ref[pl.ds(pl.multiple_of(base + 8 * g, 8), 8), pl.ds(base, HB)] for g in range(HB // 8)
        ]
        li = jnp.concatenate(invert_factor(groups, hook), axis=0)
        inv_ref[pl.ds(base, HB), pl.ds(base, HB)] = li
        for k in range(blocks):

            @pl.when(kb == k)
            def _():
                lo, hi = k * HB, (k + 1) * HB
                if k > 0:
                    inv_ref[lo:hi, :lo] = dot(li, inv_ref[lo:hi, :lo])
                for j in range(k + 1, blocks):
                    s_ref[lo:hi, j * HB : (j + 1) * HB] += lead_ref[UPPER.index((k, j))]
                if k + 1 < blocks:
                    u = dot(li, s_ref[lo:hi, hi:])
                    ut = u.T
                    s_ref[hi:, hi:] -= dot(ut, u)
                    inv_ref[hi:, :hi] -= dot(ut, inv_ref[lo:hi, :hi])

        return carry

    lax.fori_loop(0, blocks, step, 0)


def whole_kernel(
    n_row,
    n_col,
    a_ref,
    b_ref,
    out_ref,
    y_ref,
    rows_ref,
    lead_ref,
    pan_ref,
    rhs_ref,
    s_ref,
    inv_ref,
    send_sem,
    recv_sem,
):
    slots = a_ref.shape[1] // NB
    ex = Exchange(n_row, n_col, send_sem, recv_sem)
    r, c = ex.r, ex.c
    ex.barrier()
    ahead, inside = plan_exchange(
        ex, n_col, slots, a_ref, b_ref, rows_ref, lead_ref, pan_ref, rhs_ref
    )
    ahead[0]()
    s_ref[...] = jnp.zeros_like(s_ref)
    inv_ref[...] = jnp.zeros_like(inv_ref)
    for job in ahead[1:]:
        job()
    factor_lead(lead_ref, s_ref, inv_ref, inside)

    def panel(first, second):
        left = dot_nt(first, inv_ref[:NB, :NB])
        right = dot_nt(first, inv_ref[NB:, :NB]) + dot_nt(second, inv_ref[NB:, NB:])
        return left, right

    p0, p1 = panel(rows_ref[0], rows_ref[1])
    y0 = dot(inv_ref[:NB, :NB], rhs_ref[0])
    y1 = dot(inv_ref[NB:, :NB], rhs_ref[0]) + dot(inv_ref[NB:, NB:], rhs_ref[1])
    updated = b_ref[...] - (dot(p0, y0) + dot(p1, y1))
    y_ref[...] = jnp.where(r == 0, y0, jnp.where(r == 1, y1, updated))
    tri = lax.broadcasted_iota(jnp.int32, (NB, NB), 0) >= lax.broadcasted_iota(jnp.int32, (NB, NB), 1)
    for slot in range(slots):
        cols = slice(slot * NB, (slot + 1) * NB)
        j = c + n_col * slot
        inner = jnp.logical_and(r >= 2, j >= 2)

        @pl.when(inner)
        def _():
            z0, z1 = panel(pan_ref[slot, 0], pan_ref[slot, 1])
            out_ref[:, cols] = a_ref[:, cols] - (dot_nt(p0, z0) + dot_nt(p1, z1))

        @pl.when(jnp.logical_not(inner))
        def _():
            keep = jnp.logical_or(r > j, jnp.logical_and(r == j, tri))
            out_ref[:, cols] = jnp.where(keep, jnp.where(j == 0, p0, p1), 0.0)

    ex.finish()


def whole(n_row, n_col, a, b):
    vmem = pl.BlockSpec(memory_space=pltpu.VMEM)
    shapes = [
        (2, NB, NB),
        (len(UPPER), HB, HB),
        (a.shape[1] // NB, 2, NB, NB),
        (2,) + b.shape,
        (LEAD, LEAD),
        (LEAD, LEAD),
    ]
    return pl.pallas_call(
        functools.partial(whole_kernel, n_row, n_col),
        out_shape=[jax.ShapeDtypeStruct(x.shape, jnp.float32) for x in (a, b)],
        in_specs=[vmem] * 2,
        out_specs=[vmem] * 2,
        scratch_shapes=[pltpu.VMEM(s, jnp.float32) for s in shapes]
        + [pltpu.SemaphoreType.DMA((ITEMS, 3)), pltpu.SemaphoreType.DMA((ITEMS,))],
        compiler_params=pltpu.CompilerParams(
            collective_id=0, has_side_effects=True, vmem_limit_bytes=40 * 1024 * 1024
        ),
    )(a, b)


def solution(mesh):
    n_row, n_col = mesh.shape["row"], mesh.shape["col"]

    def per_device(a, b):
        return tuple(whole(n_row, n_col, a, b))

    placed = (P("row", "col"), P("row", None))
    return jax.shard_map(
        per_device, mesh=mesh, in_specs=placed, out_specs=placed, check_vma=False
    )
```

time: 104 us -> 77 us (0.74)
  the two profiles are of different devices: /device:TPU:26 before, /device:TPU:14 now
where the time goes in v3:
time: 77 us; the launch traced here: 76.8 us
  Pallas kernels  72.8 us (95%)
  local copies, waits for them, and re-layouts  3.39 us (4%)
    pallas_call x1, Pallas kernels, whole(): pl.pallas_call(functools.partial(whole_kernel, n_row, n_col), out_shape=[...  72.8 us
    unnamed x6, local copies, waits for them, and re-layouts  3.39 us

profile of v3, /device:TPU:14, one launch (start us, length us, event | category | flops | bytes accessed | tf_op | source)
XLA Modules:
  0.0 76.8 jit_solution(4028564268040104010)
XLA Ops:
  0.6 0.0 copy-start
  0.6 1.0 %copy-done = f32[256,512]{1,0:T(8,128)S(1)} copy-done((f32[256,512]{1,0:T(8,128)S(1)}, f32[256,512]{1,0:T(8,128)}, u32[]{:S(2)}) %copy-start) | copy-done | bytes 524312
  1.7 0.0 copy-start.1
  1.7 0.9 %copy-done.1 = f32[256,128]{1,0:T(8,128)S(1)} copy-done((f32[256,128]{1,0:T(8,128)S(1)}, f32[256,128]{1,0:T(8,128)}, u32[]{:S(2)}) %copy-start.1) | copy-done | bytes 131096
  2.6 72.8 %shard_map.41 = (f32[256,512]{1,0:T(8,128)S(1)}, f32[256,128]{1,0:T(8,128)S(1)}) custom-call(f32[256,512]{1,0:T(8,128)S(1)} %copy-done, f32[256,128]{1,0:T(8,128)S(1)} %copy-done.1), custom_call_target="tpu_custom_call" | custom-call | tf_op jit(solution)/shard_map/pallas_call | solution.py:370
  75.4 0.8 %copy.6 = f32[256,512]{1,0:T(8,128)} copy(f32[256,512]{1,0:T(8,128)S(1)} %get-tuple-element.4) | data formatting | bytes 1048576
  76.2 0.7 copy.7
Async XLA Ops:
  0.6 1.0 %copy-start = (f32[256,512]{1,0:T(8,128)S(1)}, f32[256,512]{1,0:T(8,128)}, u32[]{:S(2)}) copy-start(f32[256,512]{1,0:T(8,128)} %a_ref.1) | copy-start | bytes 1572868
  1.7 0.9 %copy-start.1 = (f32[256,128]{1,0:T(8,128)S(1)}, f32[256,128]{1,0:T(8,128)}, u32[]{:S(2)}) copy-start(f32[256,128]{1,0:T(8,128)} %b_ref.1) | copy-start | bytes 393220

commit v4 on v3

--- a/solution.py
+++ b/solution.py
@@ -109,6 +109,39 @@
 
         return from_source, elsewhere
 
+    def swap(self, src, dst, landing, active_out, active_in):
+        item = self.items
+        self.items += 1
+        pair = self.c + 1 - 2 * (self.c % 2)
+
+        def send():
+            @pl.when(active_out)
+            def _():
+                descriptor(src, dst).start()
+
+        def receive():
+            @pl.when(active_in)
+            def _():
+                descriptor(landing, landing).wait_recv()
+
+        def descriptor(here, there):
+            return pltpu.make_async_remote_copy(
+                src_ref=here,
+                dst_ref=there,
+                send_sem=self.send_sem.at[item, 0],
+                recv_sem=self.recv_sem.at[item],
+                device_id=self.at("col", pair),
+                device_id_type=MESH,
+            )
+
+        def wait_sent():
+            @pl.when(active_out)
+            def _():
+                descriptor(src, dst).wait_send()
+
+        self.sent.append(wait_sent)
+        return send, receive
+
     def finish(self):
         for wait_sent in self.sent:
             wait_sent()
@@ -121,10 +154,11 @@
 LEAD_ITEMS = [(0, 1, 0, 0), (1, 1, 0, 0), (2, 2, 0, 1), (4, 1, 0, 0), (5, 2, 0, 1), (7, 3, 1, 1)]
 
 
-def plan_exchange(ex, n_col, slots, a_ref, b_ref, rows_ref, lead_ref, pan_ref, rhs_ref):
+def plan_exchange(ex, n_col, slots, a_ref, b_ref, rows_ref, lead_ref, pan_ref, car_ref, rhs_ref):
     r, c = ex.r, ex.c
     halves = [pl.ds(0, HB), pl.ds(HB, HB)]
-    rows_items = [ex.flow(rows_ref.at[q], "col", q) for q in range(2)]
+    rows_early = [ex.flow(rows_ref.at[q], "col", q, active=r >= 2) for q in range(2)]
+    rows_late = [ex.flow(rows_ref.at[q], "col", q, active=r < 2) for q in range(2)]
     lead = []
     for start, count, q, owner in LEAD_ITEMS:
         ref = lead_ref.at[pl.ds(start, count)]
@@ -133,13 +167,27 @@
         (ex.flow(rhs_ref.at[q], "row", q, active=c == 2), ex.flow(rhs_ref.at[q], "col", 2))
         for q in range(2)
     ]
+    q = c % 2
+    pair = c + 1 - 2 * q
     pan = []
-    for q in range(2):
-        for half in halves:
-            for t in range(slots):
-                j = c + n_col * t
-                active = jnp.logical_and(r >= 2, j >= 2)
-                pan.append(ex.flow(pan_ref.at[t, q, half], "row", j, low=2, active=active))
+    for half in halves:
+        for t in range(slots):
+            j, j_pair = c + n_col * t, pair + n_col * t
+            own = jnp.logical_and(r >= 2, j >= 2)
+            other = jnp.logical_and(r >= 2, j_pair >= 2)
+            pan.append(
+                (
+                    ex.flow(pan_ref.at[t, q, half], "row", j, low=2, active=own),
+                    ex.flow(car_ref.at[t, half], "row", j_pair, low=2, active=other),
+                    ex.swap(
+                        car_ref.at[t, half],
+                        pan_ref.at[t, q, half],
+                        pan_ref.at[t, 1 - q, half],
+                        jnp.logical_and(other, r != j_pair),
+                        jnp.logical_and(own, r != j),
+                    ),
+                )
+            )
 
     def start():
         for n, (i, j) in enumerate(UPPER):
@@ -157,7 +205,7 @@
             def _():
                 rows_ref[q] = a_ref[:, :NB]
 
-            rows_items[q][0]()
+            rows_early[q][0]()
 
             @pl.when(jnp.logical_and(r == q, c == 2))
             def _():
@@ -169,15 +217,39 @@
         pair[0][1]()
         pair[1][0]()
 
-    def start_pan():
+    def start_pan(native):
+        here = jnp.logical_and(r >= 2, c < 2 if native else c >= 2)
         for t in range(slots):
 
+            @pl.when(jnp.logical_and(here, r == c + n_col * t))
+            def _():
+                pan_ref[t, q] = a_ref[:, :NB] if native else rows_ref[q]
+
+            @pl.when(jnp.logical_and(here, r == pair + n_col * t))
+            def _():
+                car_ref[t] = a_ref[:, :NB] if native else rows_ref[q]
+
+        @pl.when(here)
+        def _():
+            for own, other, _ in pan:
+                own[0]()
+                other[0]()
+
+    def own_pan():
+        for t in range(slots):
+
             @pl.when(jnp.logical_and(r >= 2, r == c + n_col * t))
             def _():
-                pan_ref[t] = rows_ref[...]
-
-        for item in pan:
-            item[0]()
+                pan_ref[t, 1 - q] = rows_ref[1 - q]
+
+    def pan_row(n):
+        def run():
+            own, other, swap = pan[n]
+            own[1]()
+            other[1]()
+            swap[0]()
+
+        return run
 
     inside = {}
 
@@ -190,17 +262,22 @@
     def along_col(n):
         return lead[n][1][1]
 
-    ahead = [start, along_row(0), along_col(0)]
+    ahead = [start, lambda: start_pan(True), along_row(0), along_col(0)]
     put(0, along_row(1), along_row(2))
-    put(1, along_col(1), along_col(2), rows_items[0][1], rows_items[1][1], start_pan)
+    put(1, along_col(1), along_col(2), rows_early[0][1], rows_early[1][1])
+    put(1, lambda: start_pan(False), own_pan)
     put(2, along_row(3), along_row(4))
     put(3, along_col(3), along_col(4))
     put(4, along_row(5))
     put(5, along_col(5))
     put(6, lambda: pass_on(rhs[0]), lambda: pass_on(rhs[1]))
     put(8, rhs[0][1][1], rhs[1][1][1])
+    put(5, rows_late[0][0], rows_late[1][0])
+    put(10, rows_late[0][1], rows_late[1][1])
     for n, item in enumerate(pan):
-        put(5 + n * 8 // len(pan), item[1])
+        at = 5 + n * 8 // len(pan)
+        put(at, pan_row(n))
+        put(at + 3, item[2][1])
     return ahead, inside
 
 
@@ -308,6 +385,7 @@
     rows_ref,
     lead_ref,
     pan_ref,
+    car_ref,
     rhs_ref,
     s_ref,
     inv_ref,
@@ -319,7 +397,7 @@
     r, c = ex.r, ex.c
     ex.barrier()
     ahead, inside = plan_exchange(
-        ex, n_col, slots, a_ref, b_ref, rows_ref, lead_ref, pan_ref, rhs_ref
+        ex, n_col, slots, a_ref, b_ref, rows_ref, lead_ref, pan_ref, car_ref, rhs_ref
     )
     ahead[0]()
     s_ref[...] = jnp.zeros_like(s_ref)
@@ -363,6 +441,7 @@
         (2, NB, NB),
         (len(UPPER), HB, HB),
         (a.shape[1] // NB, 2, NB, NB),
+        (a.shape[1] // NB, NB, NB),
         (2,) + b.shape,
         (LEAD, LEAD),
         (LEAD, LEAD),

time: 77 us -> 98.9 us (1.28)
  the two profiles are of different devices: /device:TPU:14 before, /device:TPU:10 now
where the time goes in v4:
time: 98.9 us; the launch traced here: 98.7 us
  Pallas kernels  94.7 us (96%)
  local copies, waits for them, and re-layouts  3.39 us (3%)
    pallas_call x1, Pallas kernels, whole(): pl.pallas_call(functools.partial(whole_kernel, n_row, n_col), out_shape=[...  94.7 us
    unnamed x6, local copies, waits for them, and re-layouts  3.39 us

profile of v4, /device:TPU:10, one launch (start us, length us, event | category | flops | bytes accessed | tf_op | source)
XLA Modules:
  0.0 98.7 jit_solution(12576025327389957626)
XLA Ops:
  0.6 0.0 copy-start
  0.6 1.0 %copy-done = f32[256,512]{1,0:T(8,128)S(1)} copy-done((f32[256,512]{1,0:T(8,128)S(1)}, f32[256,512]{1,0:T(8,128)}, u32[]{:S(2)}) %copy-start) | copy-done | bytes 524312
  1.7 0.0 copy-start.1
  1.7 0.9 copy-done.1
  2.6 94.7 %shard_map.41 = (f32[256,512]{1,0:T(8,128)S(1)}, f32[256,128]{1,0:T(8,128)S(1)}) custom-call(f32[256,512]{1,0:T(8,128)S(1)} %copy-done, f32[256,128]{1,0:T(8,128)S(1)} %copy-done.1), custom_call_target="tpu_custom_call" | custom-call | tf_op jit(solution)/shard_map/pallas_call | solution.py:449
  97.3 0.8 copy.6
  98.1 0.7 copy.7
Async XLA Ops:
  0.6 1.0 %copy-start = (f32[256,512]{1,0:T(8,128)S(1)}, f32[256,512]{1,0:T(8,128)}, u32[]{:S(2)}) copy-start(f32[256,512]{1,0:T(8,128)} %a_ref.1) | copy-start | bytes 1572868
  1.7 0.9 copy-start.1

commit v5 on v3

--- a/solution.py
+++ b/solution.py
@@ -115,7 +115,6 @@
 
 
 ITEMS = 48
-POINTS = 4
 BLOCKS = LEAD // HB
 UPPER = [(i, j) for i in range(BLOCKS) for j in range(i, BLOCKS)]
 LEAD_ITEMS = [(0, 1, 0, 0), (1, 1, 0, 0), (2, 2, 0, 1), (4, 1, 0, 0), (5, 2, 0, 1), (7, 3, 1, 1)]
@@ -208,15 +207,13 @@
     return jnp.broadcast_to(x[j : j + 1, :], x.shape)
 
 
-def invert_factor(s, hook=lambda point: None):
+def invert_factor(s):
     sub = lax.broadcasted_iota(jnp.int32, (8, HB), 0)
     lane = lax.broadcasted_iota(jnp.int32, (8, HB), 1)
     groups = len(s)
     t = [jnp.where(lane == sub + 8 * h, 1.0, 0.0).astype(jnp.float32) for h in range(groups)]
     done = []
     for g in range(groups):
-        if g % (groups // POINTS) == 0:
-            hook(g // (groups // POINTS))
         p, q, f = s[g], t[g], t[g]
         lanes = [jnp.broadcast_to(p[:, 8 * g + k : 8 * g + k + 1], (8, HB)) for k in range(8)]
         scale = jnp.ones((8, HB), jnp.float32)
@@ -251,20 +248,10 @@
     return done
 
 
-def factor_lead(lead_ref, s_ref, inv_ref, inside):
+def factor_lead(lead_ref, s_ref, inv_ref):
     blocks = BLOCKS
 
     def step(kb, carry):
-        def hook(point):
-            for k in range(blocks):
-                jobs = inside.get(k * POINTS + point)
-                if jobs:
-
-                    @pl.when(kb == k)
-                    def _():
-                        for job in jobs:
-                            job()
-
         base = pl.multiple_of(kb * HB, HB)
         for k in range(blocks):
 
@@ -276,7 +263,7 @@
         groups = [
             s_ref[pl.ds(pl.multiple_of(base + 8 * g, 8), 8), pl.ds(base, HB)] for g in range(HB // 8)
         ]
-        li = jnp.concatenate(invert_factor(groups, hook), axis=0)
+        li = jnp.concatenate(invert_factor(groups), axis=0)
         inv_ref[pl.ds(base, HB), pl.ds(base, HB)] = li
         for k in range(blocks):
 
@@ -326,7 +313,10 @@
     inv_ref[...] = jnp.zeros_like(inv_ref)
     for job in ahead[1:]:
         job()
-    factor_lead(lead_ref, s_ref, inv_ref, inside)
+    for point in sorted(inside):
+        for job in inside[point]:
+            job()
+    factor_lead(lead_ref, s_ref, inv_ref)
 
     def panel(first, second):
         left = dot_nt(first, inv_ref[:NB, :NB])

time: 77 us -> 88.2 us (1.15)
  the two profiles are of different devices: /device:TPU:14 before, /device:TPU:28 now
where the time goes in v5:
time: 88.2 us; the launch traced here: 88 us
  Pallas kernels  84 us (95%)
  local copies, waits for them, and re-layouts  3.39 us (4%)
    pallas_call x1, Pallas kernels, whole(): pl.pallas_call(functools.partial(whole_kernel, n_row, n_col), out_shape=[...  84 us
    unnamed x6, local copies, waits for them, and re-layouts  3.39 us

profile of v5, /device:TPU:28, one launch (start us, length us, event | category | flops | bytes accessed | tf_op | source)
XLA Modules:
  0.0 88.0 jit_solution(17787716738252576421)
XLA Ops:
  0.6 0.0 copy-start
  0.6 1.0 %copy-done = f32[256,512]{1,0:T(8,128)S(1)} copy-done((f32[256,512]{1,0:T(8,128)S(1)}, f32[256,512]{1,0:T(8,128)}, u32[]{:S(2)}) %copy-start) | copy-done | bytes 524312
  1.7 0.0 copy-start.1
  1.7 0.9 %copy-done.1 = f32[256,128]{1,0:T(8,128)S(1)} copy-done((f32[256,128]{1,0:T(8,128)S(1)}, f32[256,128]{1,0:T(8,128)}, u32[]{:S(2)}) %copy-start.1) | copy-done | bytes 131096
  2.6 84.0 %shard_map.41 = (f32[256,512]{1,0:T(8,128)S(1)}, f32[256,128]{1,0:T(8,128)S(1)}) custom-call(f32[256,512]{1,0:T(8,128)S(1)} %copy-done, f32[256,128]{1,0:T(8,128)S(1)} %copy-done.1), custom_call_target="tpu_custom_call" | custom-call | tf_op jit(solution)/shard_map/pallas_call | solution.py:360
  86.6 0.8 copy.6
  87.4 0.7 copy.7
Async XLA Ops:
  0.6 1.0 %copy-start = (f32[256,512]{1,0:T(8,128)S(1)}, f32[256,512]{1,0:T(8,128)}, u32[]{:S(2)}) copy-start(f32[256,512]{1,0:T(8,128)} %a_ref.1) | copy-start | bytes 1572868
  1.7 0.9 %copy-start.1 = (f32[256,128]{1,0:T(8,128)S(1)}, f32[256,128]{1,0:T(8,128)}, u32[]{:S(2)}) copy-start(f32[256,128]{1,0:T(8,128)} %b_ref.1) | copy-start | bytes 393220

commit v6 on v3

--- a/solution.py
+++ b/solution.py
@@ -69,15 +69,17 @@
             device_id_type=MESH,
         )
 
-    def flow(self, ref, axis, source, low=0, active=True):
+    def flow(self, ref, axis, source, low=0, active=True, cross=False):
         me, size = self.axes[axis]
+        root = source + 1 - 2 * (source % 2) if cross else source
         item = self.items
         self.items += 1
-        chain = jnp.logical_and(active, me % 2 == source % 2)
+        chain = jnp.logical_and(active, me % 2 == root % 2)
+        to_pair = jnp.logical_or(me == source, jnp.logical_and(chain, me // 2 != source // 2))
         sends = (
-            (jnp.logical_and(chain, jnp.logical_and(me >= source, me + 2 < size)), me + 2),
-            (jnp.logical_and(chain, jnp.logical_and(me <= source, me >= low + 2)), me - 2),
-            (chain, me + 1 - 2 * (me % 2)),
+            (jnp.logical_and(chain, jnp.logical_and(me >= root, me + 2 < size)), me + 2),
+            (jnp.logical_and(chain, jnp.logical_and(me <= root, me >= low + 2)), me - 2),
+            (jnp.logical_and(active, to_pair), me + 1 - 2 * (me % 2)),
         )
 
         def send():
@@ -124,7 +126,8 @@
 def plan_exchange(ex, n_col, slots, a_ref, b_ref, rows_ref, lead_ref, pan_ref, rhs_ref):
     r, c = ex.r, ex.c
     halves = [pl.ds(0, HB), pl.ds(HB, HB)]
-    rows_items = [ex.flow(rows_ref.at[q], "col", q) for q in range(2)]
+    rows_early = [ex.flow(rows_ref.at[q], "col", q, active=r >= 2) for q in range(2)]
+    rows_late = [ex.flow(rows_ref.at[q], "col", q, active=r < 2) for q in range(2)]
     lead = []
     for start, count, q, owner in LEAD_ITEMS:
         ref = lead_ref.at[pl.ds(start, count)]
@@ -135,11 +138,12 @@
     ]
     pan = []
     for q in range(2):
-        for half in halves:
+        for h, half in enumerate(halves):
             for t in range(slots):
                 j = c + n_col * t
                 active = jnp.logical_and(r >= 2, j >= 2)
-                pan.append(ex.flow(pan_ref.at[t, q, half], "row", j, low=2, active=active))
+                ref = pan_ref.at[t, q, half]
+                pan.append(ex.flow(ref, "row", j, low=2, active=active, cross=h == 1))
 
     def start():
         for n, (i, j) in enumerate(UPPER):
@@ -157,7 +161,7 @@
             def _():
                 rows_ref[q] = a_ref[:, :NB]
 
-            rows_items[q][0]()
+            rows_early[q][0]()
 
             @pl.when(jnp.logical_and(r == q, c == 2))
             def _():
@@ -192,13 +196,15 @@
 
     ahead = [start, along_row(0), along_col(0)]
     put(0, along_row(1), along_row(2))
-    put(1, along_col(1), along_col(2), rows_items[0][1], rows_items[1][1], start_pan)
+    put(1, along_col(1), along_col(2), rows_early[0][1], rows_early[1][1], start_pan)
     put(2, along_row(3), along_row(4))
     put(3, along_col(3), along_col(4))
     put(4, along_row(5))
     put(5, along_col(5))
     put(6, lambda: pass_on(rhs[0]), lambda: pass_on(rhs[1]))
     put(8, rhs[0][1][1], rhs[1][1][1])
+    put(5, rows_late[0][0], rows_late[1][0])
+    put(10, rows_late[0][1], rows_late[1][1])
     for n, item in enumerate(pan):
         put(5 + n * 8 // len(pan), item[1])
     return ahead, inside

time: 77 us -> 123 us (1.60)
  the two profiles are of different devices: /device:TPU:14 before, /device:TPU:10 now
where the time goes in v6:
time: 123 us; the launch traced here: 122 us
  Pallas kernels  118 us (96%)
  local copies, waits for them, and re-layouts  3.39 us (3%)
    pallas_call x1, Pallas kernels, whole(): pl.pallas_call(functools.partial(whole_kernel, n_row, n_col), out_shape=[...  118 us
    unnamed x6, local copies, waits for them, and re-layouts  3.39 us

profile of v6, /device:TPU:10, one launch (start us, length us, event | category | flops | bytes accessed | tf_op | source)
XLA Modules:
  0.0 122.4 jit_solution(14745533952447300744)
XLA Ops:
  0.6 0.0 copy-start
  0.6 1.0 copy-done
  1.7 0.0 copy-start.1
  1.7 0.9 copy-done.1
  2.6 118.4 %shard_map.41 = (f32[256,512]{1,0:T(8,128)S(1)}, f32[256,128]{1,0:T(8,128)S(1)}) custom-call(f32[256,512]{1,0:T(8,128)S(1)} %copy-done, f32[256,128]{1,0:T(8,128)S(1)} %copy-done.1), custom_call_target="tpu_custom_call" | custom-call | tf_op jit(solution)/shard_map/pallas_call | solution.py:376
  121.0 0.8 copy.6
  121.7 0.7 copy.7
Async XLA Ops:
  0.6 1.0 copy-start
  1.7 0.9 copy-start.1

commit v7 on v6

--- a/solution.py
+++ b/solution.py
@@ -44,6 +44,8 @@
                 (None, me + 1 - 2 * (me % 2)),
                 (me + 2 < size, me + 2),
                 (me >= 2, me - 2),
+                (me + 4 < size, me + 4),
+                (me >= 4, me - 4),
             ):
 
                 def signal():
@@ -69,18 +71,26 @@
             device_id_type=MESH,
         )
 
-    def flow(self, ref, axis, source, low=0, active=True, cross=False):
+    def flow(self, ref, axis, source, low=0, active=True, far=False):
         me, size = self.axes[axis]
-        root = source + 1 - 2 * (source % 2) if cross else source
         item = self.items
         self.items += 1
-        chain = jnp.logical_and(active, me % 2 == root % 2)
-        to_pair = jnp.logical_or(me == source, jnp.logical_and(chain, me // 2 != source // 2))
-        sends = (
-            (jnp.logical_and(chain, jnp.logical_and(me >= root, me + 2 < size)), me + 2),
-            (jnp.logical_and(chain, jnp.logical_and(me <= root, me >= low + 2)), me - 2),
-            (jnp.logical_and(active, to_pair), me + 1 - 2 * (me % 2)),
-        )
+        chain = jnp.logical_and(active, me % 2 == source % 2)
+        up = jnp.logical_and(chain, me >= source)
+        down = jnp.logical_and(chain, me <= source)
+        ahead = []
+        if far:
+            relay = (me // 2 + source // 2) % 2 == 0
+            up, down = jnp.logical_and(up, relay), jnp.logical_and(down, relay)
+            ahead = [
+                (jnp.logical_and(up, me + 4 < size), me + 4),
+                (jnp.logical_and(down, me >= low + 4), me - 4),
+            ]
+        sends = ahead + [
+            (jnp.logical_and(up, me + 2 < size), me + 2),
+            (jnp.logical_and(down, me >= low + 2), me - 2),
+            (chain, me + 1 - 2 * (me % 2)),
+        ]
 
         def send():
             for way, (there, target) in enumerate(sends):
@@ -138,12 +148,11 @@
     ]
     pan = []
     for q in range(2):
-        for h, half in enumerate(halves):
+        for half in halves:
             for t in range(slots):
                 j = c + n_col * t
                 active = jnp.logical_and(r >= 2, j >= 2)
-                ref = pan_ref.at[t, q, half]
-                pan.append(ex.flow(ref, "row", j, low=2, active=active, cross=h == 1))
+                pan.append(ex.flow(pan_ref.at[t, q, half], "row", j, low=2, active=active, far=True))
 
     def start():
         for n, (i, j) in enumerate(UPPER):
@@ -379,7 +388,7 @@
         in_specs=[vmem] * 2,
         out_specs=[vmem] * 2,
         scratch_shapes=[pltpu.VMEM(s, jnp.float32) for s in shapes]
-        + [pltpu.SemaphoreType.DMA((ITEMS, 3)), pltpu.SemaphoreType.DMA((ITEMS,))],
+        + [pltpu.SemaphoreType.DMA((ITEMS, 5)), pltpu.SemaphoreType.DMA((ITEMS,))],
         compiler_params=pltpu.CompilerParams(
             collective_id=0, has_side_effects=True, vmem_limit_bytes=40 * 1024 * 1024
         ),

time: 123 us -> 76.6 us (0.62)
  the two profiles are of different devices: /device:TPU:10 before, /device:TPU:30 now
where the time goes in v7:
time: 76.6 us; the launch traced here: 76.4 us
  Pallas kernels  72.4 us (95%)
  local copies, waits for them, and re-layouts  3.39 us (4%)
    pallas_call x1, Pallas kernels, whole(): pl.pallas_call(functools.partial(whole_kernel, n_row, n_col), out_shape=[...  72.4 us
    unnamed x6, local copies, waits for them, and re-layouts  3.39 us

profile of v7, /device:TPU:30, one launch (start us, length us, event | category | flops | bytes accessed | tf_op | source)
XLA Modules:
  0.0 76.4 jit_solution(15399415844431591298)
XLA Ops:
  0.6 0.0 copy-start
  0.6 1.0 %copy-done = f32[256,512]{1,0:T(8,128)S(1)} copy-done((f32[256,512]{1,0:T(8,128)S(1)}, f32[256,512]{1,0:T(8,128)}, u32[]{:S(2)}) %copy-start) | copy-done | bytes 524312
  1.7 0.0 copy-start.1
  1.7 0.9 %copy-done.1 = f32[256,128]{1,0:T(8,128)S(1)} copy-done((f32[256,128]{1,0:T(8,128)S(1)}, f32[256,128]{1,0:T(8,128)}, u32[]{:S(2)}) %copy-start.1) | copy-done | bytes 131096
  2.6 72.4 %shard_map.41 = (f32[256,512]{1,0:T(8,128)S(1)}, f32[256,128]{1,0:T(8,128)S(1)}) custom-call(f32[256,512]{1,0:T(8,128)S(1)} %copy-done, f32[256,128]{1,0:T(8,128)S(1)} %copy-done.1), custom_call_target="tpu_custom_call" | custom-call | tf_op jit(solution)/shard_map/pallas_call | solution.py:385
  75.0 0.8 %copy.6 = f32[256,512]{1,0:T(8,128)} copy(f32[256,512]{1,0:T(8,128)S(1)} %get-tuple-element.4) | data formatting | bytes 1048576
  75.8 0.7 copy.7
Async XLA Ops:
  0.6 1.0 %copy-start = (f32[256,512]{1,0:T(8,128)S(1)}, f32[256,512]{1,0:T(8,128)}, u32[]{:S(2)}) copy-start(f32[256,512]{1,0:T(8,128)} %a_ref.1) | copy-start | bytes 1572868
  1.7 0.9 %copy-start.1 = (f32[256,128]{1,0:T(8,128)S(1)}, f32[256,128]{1,0:T(8,128)}, u32[]{:S(2)}) copy-start(f32[256,128]{1,0:T(8,128)} %b_ref.1) | copy-start | bytes 393220

commit v8 on v7

--- a/solution.py
+++ b/solution.py
@@ -170,8 +170,6 @@
             def _():
                 rows_ref[q] = a_ref[:, :NB]
 
-            rows_early[q][0]()
-
             @pl.when(jnp.logical_and(r == q, c == 2))
             def _():
                 rhs_ref[q] = b_ref[...]
@@ -204,18 +202,16 @@
         return lead[n][1][1]
 
     ahead = [start, along_row(0), along_col(0)]
-    put(0, along_row(1), along_row(2))
-    put(1, along_col(1), along_col(2), rows_early[0][1], rows_early[1][1], start_pan)
-    put(2, along_row(3), along_row(4))
-    put(3, along_col(3), along_col(4))
-    put(4, along_row(5))
-    put(5, along_col(5))
+    put(0, along_row(1), along_row(2), rows_early[0][0], rows_early[1][0])
+    put(1, along_col(1), along_col(2), along_row(3), along_row(4))
+    put(2, along_col(3), along_col(4), along_row(5))
+    put(4, along_col(5))
+    put(5, rows_early[0][1], rows_early[1][1], start_pan, rows_late[0][0], rows_late[1][0])
     put(6, lambda: pass_on(rhs[0]), lambda: pass_on(rhs[1]))
     put(8, rhs[0][1][1], rhs[1][1][1])
-    put(5, rows_late[0][0], rows_late[1][0])
     put(10, rows_late[0][1], rows_late[1][1])
     for n, item in enumerate(pan):
-        put(5 + n * 8 // len(pan), item[1])
+        put(8 + n * 8 // len(pan), item[1])
     return ahead, inside
 
 

time: 76.6 us -> 82.9 us (1.082)
  Pallas kernels: 72.4 us -> 78.7 us
    pallas_call x1, Pallas kernels: 72.4 us -> 78.7 us  [whole(): pl.pallas_call(functools.partial(whole_kernel, n_row, n_col), out_shape=[...]
where the time goes in v8:
time: 82.9 us; the launch traced here: 82.7 us
  Pallas kernels  78.7 us (95%)
  local copies, waits for them, and re-layouts  3.39 us (4%)
    pallas_call x1, Pallas kernels, whole(): pl.pallas_call(functools.partial(whole_kernel, n_row, n_col), out_shape=[...  78.7 us
    unnamed x6, local copies, waits for them, and re-layouts  3.39 us

profile of v8, /device:TPU:30, one launch (start us, length us, event | category | flops | bytes accessed | tf_op | source)
XLA Modules:
  0.0 82.7 jit_solution(12755660794192899767)
XLA Ops:
  0.6 0.0 copy-start
  0.6 1.0 %copy-done = f32[256,512]{1,0:T(8,128)S(1)} copy-done((f32[256,512]{1,0:T(8,128)S(1)}, f32[256,512]{1,0:T(8,128)}, u32[]{:S(2)}) %copy-start) | copy-done | bytes 524312
  1.7 0.0 copy-start.1
  1.7 0.9 %copy-done.1 = f32[256,128]{1,0:T(8,128)S(1)} copy-done((f32[256,128]{1,0:T(8,128)S(1)}, f32[256,128]{1,0:T(8,128)}, u32[]{:S(2)}) %copy-start.1) | copy-done | bytes 131096
  2.6 78.7 %shard_map.41 = (f32[256,512]{1,0:T(8,128)S(1)}, f32[256,128]{1,0:T(8,128)S(1)}) custom-call(f32[256,512]{1,0:T(8,128)S(1)} %copy-done, f32[256,128]{1,0:T(8,128)S(1)} %copy-done.1), custom_call_target="tpu_custom_call" | custom-call | tf_op jit(solution)/shard_map/pallas_call | solution.py:381
  81.3 0.8 copy.6
  82.1 0.7 copy.7
Async XLA Ops:
  0.6 1.0 %copy-start = (f32[256,512]{1,0:T(8,128)S(1)}, f32[256,512]{1,0:T(8,128)}, u32[]{:S(2)}) copy-start(f32[256,512]{1,0:T(8,128)} %a_ref.1) | copy-start | bytes 1572868
  1.7 0.9 %copy-start.1 = (f32[256,128]{1,0:T(8,128)S(1)}, f32[256,128]{1,0:T(8,128)}, u32[]{:S(2)}) copy-start(f32[256,128]{1,0:T(8,128)} %b_ref.1) | copy-start | bytes 393220
